TPU v7x, 512 devices: a whole 4x4x16 slice. The times are simulated.
512 devices in a mesh: replica: 32 (over z, y_lo), fsdp: 16 (over x, y_hi, core).
Axes of the slice: x: 4, y: 4 (y_hi: 2, y_lo: 2; y = y_hi * 2 + y_lo), z: 16, core: 2. Of those that a mesh axis runs over, the one named last changes fastest.
Arguments:
- tokens: bfloat16 [32, 2048, 4096], P('replica', 'fsdp'), may hold values from -6 to 6
- local_weight: bfloat16 [32, 4096, 512], P('replica', 'fsdp'), may hold values from -6 to 6
- key_cot: bfloat16 [32, 2048, 512], P('replica', 'fsdp'), may hold values from -6 to 6
- global_weight: float32 [4096, 512], P(('fsdp', 'replica')), may hold values from -6 to 6
- momentum: float32 [4096, 512], P(('fsdp', 'replica')), may hold values from -6 to 6
- anchor: float32 [4096, 512], P(('fsdp', 'replica')), may hold values from -6 to 6
Outputs:
- keys: bfloat16 [32, 2048, 512], P('replica', 'fsdp')
- grad_tokens: bfloat16 [32, 2048, 4096], P('replica', 'fsdp')
- grad_weight: bfloat16 [32, 4096, 512], P('replica', 'fsdp')
- momentum_new: float32 [4096, 512], P(('fsdp', 'replica'))
- global_new: float32 [4096, 512], P(('fsdp', 'replica'))
- synced: bfloat16 [4096, 512], P('fsdp')
All inputs are finite; a program needn't handle non-finite values.
Results may differ from a plain program's by a relative error of at most 0.0095.
Values may be sent and summed in bfloat16 or wider, within the bound.
A program may use at most 64 MiB of HBM per device.

v0:
```python
import jax
import jax.numpy as jnp
from jax import lax
from jax.sharding import PartitionSpec as P

D_WIN = 4096


def on_device(tokens, local_weight, key_cot, global_weight, momentum, anchor):
    scale = 1.0 / D_WIN**0.5
    inputs = tokens[0]
    weight = local_weight[0]
    cot = key_cot[0]
    total = lax.psum_scatter(
        weight.astype(jnp.float32).astype(jnp.bfloat16), "replica", scatter_dimension=0, tiled=True
    ).astype(jnp.float32)
    pseudo = global_weight - total / lax.axis_size("replica")
    push = pseudo + 0.1 * (global_weight - anchor)
    momentum_new = 0.9 * momentum + push
    global_new = global_weight - 0.7 * (push + 0.9 * momentum_new)
    synced = lax.all_gather(global_new.astype(jnp.bfloat16), "replica", axis=0, tiled=True)
    columns_all = lax.all_to_all(inputs, "fsdp", split_axis=1, concat_axis=0, tiled=True)
    cot_all = lax.all_gather(cot, "fsdp", axis=0, tiled=True)
    wgrad = lax.dot_general(
        columns_all, cot_all, (((0,), (0,)), ((), ())), preferred_element_type=jnp.float32
    )
    grad_weight = (wgrad * scale).astype(jnp.bfloat16)
    piece = lax.all_gather(weight, "fsdp", axis=0, tiled=True)
    key_total = jnp.dot(inputs, piece, preferred_element_type=jnp.float32)
    part = lax.dot_general(cot, piece, (((1,), (1,)), ((), ())), preferred_element_type=jnp.float32)
    back_full = part
    summed, back_full = (key_total, back_full)
    keys = (summed * scale).astype(jnp.bfloat16)
    grad_tokens = (back_full * scale).astype(jnp.bfloat16)
    return (keys[None], grad_tokens[None], grad_weight[None], momentum_new, global_new, synced)


def solution(mesh):
    in_specs = (
        P("replica", "fsdp", None),
        P("replica", "fsdp", None),
        P("replica", "fsdp", None),
        P(("fsdp", "replica"), None),
        P(("fsdp", "replica"), None),
        P(("fsdp", "replica"), None),
    )
    out_specs = (
        P("replica", "fsdp", None),
        P("replica", "fsdp", None),
        P("replica", "fsdp", None),
        P(("fsdp", "replica"), None),
        P(("fsdp", "replica"), None),
        P("fsdp", None),
    )
    return jax.shard_map(
        on_device, mesh=mesh, in_specs=in_specs, out_specs=out_specs, check_vma=False
    )
```

profile of v0, /device:TPU:16, one launch (start us, length us, event | category | flops | bytes accessed | tf_op | source)
XLA Modules:
  0.0 245.4 jit_solution(13214008306867970524)
XLA Ops:
  8.0 0.0 copy-start.3
  8.0 0.0 copy-start.4
  8.0 0.0 copy-start.5
  8.0 0.0 reduce-scatter.2.cloned.1.call-start
  8.1 0.7 reduce-scatter.2.cloned.1.call-update
  8.8 0.0 all-gather.7.cloned.1.call-start
  8.8 0.5 all-gather.7.cloned.1.call-update
  9.3 0.0 all-gather.5.cloned.1.call-start
  9.4 0.5 all-gather.5.cloned.1.call-update
  9.9 2.3 copy.12
  12.2 0.0 copy-start.1
  12.2 9.3 %all-to-all-start = ((bf16[128,16,256]{0,2,1:T(8,128)(2,1)}), bf16[128,16,256]{0,2,1:T(8,128)(2,1)S(1)}, u32[]{:S(2)}, u32[]{:S(2)}) async-start(bf16[128,16,256]{0,2,1:T(8,128)(2,1)} %bitcast.5), calls=%async_computation | async-start | bytes 2097152 | tf_op jit(solution)/shard_map/all_to_all | solution.py:22
  21.5 142.5 %reduce-scatter.2.cloned.1.call-done = bf16[8,512]{1,0:T(8,128)(2,1)} async-done(((bf16[256,512]{1,0:T(8,128)(2,1)}), bf16[8,512]{1,0:T(8,128)(2,1)}) %reduce-scatter.2.cloned.1.call-update) | async-done | bytes 8208 | tf_op jit(solution)/shard_map/reduce_scatter | solution.py:14
  164.0 0.0 copy-done.3
  164.0 0.0 copy-done.4
  164.0 0.0 copy-done.5
  164.0 1.3 fusion.27
  165.4 62.1 %all_gather.11 = bf16[256,512]{1,0:T(8,128)(2,1)S(1)} all-gather(bf16[8,512]{1,0:T(8,128)(2,1)S(1)} %get-tuple-element.6), channel_id=1, replica_groups=mesh['replica'=32,'fsdp'=16] {'replica'}, dimensions={0}, use_global_device_ids=true | all-gather | bytes 270336 | tf_op jit(solution)/shard_map/all_gather | solution.py:21
  227.4 0.0 all-to-all-done
  227.4 0.5 copy.13
  228.0 0.0 all-gather.7.cloned.1.call-done
  228.0 0.0 copy-start.2
  228.0 3.1 %fusion.13 = bf16[1,256,512]{2,1,0:T(8,128)(2,1)} fusion(bf16[2048,256]{1,0:T(8,128)(2,1)S(1)} %bitcast.38, bf16[1,2048,512]{2,1,0:T(8,128)(2,1)} %all-gather.7.cloned.1.call-done), kind=kOutput, calls=%fused_computation.10 | convolution fusion | flops 537133056 | bytes 3407872 | tf_op jit(solution)/shard_map/dot_general | solution.py:24
  231.1 0.0 all-gather.5.cloned.1.call-done
  231.1 0.0 copy-done.1
  231.1 0.0 copy-start
  231.1 3.7 %fusion.22 = bf16[1,128,512]{2,1,0:T(8,128)(2,1)} fusion(bf16[1,4096,512]{2,1,0:T(8,128)(2,1)} %all-gather.5.cloned.1.call-done, bf16[1,128,4096]{2,1,0:T(8,128)(2,1)S(1)} %copy-done.1), kind=kOutput, calls=%fused_computation.13 | convolution fusion | flops 537001984 | bytes 5373952 | tf_op jit(solution)/shard_map/dot_general | solution.py:29
  234.8 0.0 copy-done.2
  234.8 0.0 copy-done
  234.8 2.5 %fusion.1 = bf16[1,128,4096]{2,1,0:T(8,128)(2,1)} fusion(bf16[1,4096,512]{2,1,0:T(8,128)(2,1)S(1)} %copy-done, bf16[1,128,512]{2,1,0:T(8,128)(2,1)S(1)} %copy-done.2), kind=kOutput, calls=%fused_computation.2 | convolution fusion | flops 537919488 | bytes 5373952 | tf_op jit(solution)/shard_map/dot_general | solution.py:30
  237.2 0.7 copy.15
Async XLA Ops:
  8.0 156.0 %copy-start.3 = (f32[8,512]{1,0:T(8,128)S(1)}, f32[8,512]{1,0:T(8,128)}, u32[]{:S(2)}) copy-start(f32[8,512]{1,0:T(8,128)} %param.9) | copy-start | bytes 49156
  8.0 156.0 %copy-start.4 = (f32[8,512]{1,0:T(8,128)S(1)}, f32[8,512]{1,0:T(8,128)}, u32[]{:S(2)}) copy-start(f32[8,512]{1,0:T(8,128)} %param.11) | copy-start | bytes 49156
  8.0 156.0 %copy-start.5 = (f32[8,512]{1,0:T(8,128)S(1)}, f32[8,512]{1,0:T(8,128)}, u32[]{:S(2)}) copy-start(f32[8,512]{1,0:T(8,128)} %param.10) | copy-start | bytes 49156
  8.0 156.0 %reduce-scatter.2.cloned.1.call-start = ((), (), s32[]{:S(2)}) async-start(), calls=%async_computation.2 | async-start | bytes 270336 | tf_op jit(solution)/shard_map/reduce_scatter | solution.py:14
  8.8 219.2 %all-gather.7.cloned.1.call-start = ((), (), s32[]{:S(2)}) async-start(), calls=%async_computation.4 | async-start | bytes 2228224 | tf_op jit(solution)/shard_map/all_gather | solution.py:23
  9.3 221.7 %all-gather.5.cloned.1.call-start = ((), (), s32[]{:S(2)}) async-start(), calls=%async_computation.3 | async-start | bytes 4456448 | tf_op jit(solution)/shard_map/all_gather | solution.py:28
  12.2 218.9 %copy-start.1 = (bf16[1,128,4096]{2,1,0:T(8,128)(2,1)S(1)}, bf16[1,128,4096]{2,1,0:T(8,128)(2,1)}, u32[]{:S(2)}) copy-start(bf16[1,128,4096]{2,1,0:T(8,128)(2,1)} %param.6) | copy-start | bytes 3145732
  12.2 215.2 %all-to-all-start = ((bf16[128,16,256]{0,2,1:T(8,128)(2,1)}), bf16[128,16,256]{0,2,1:T(8,128)(2,1)S(1)}, u32[]{:S(2)}, u32[]{:S(2)}) async-start(bf16[128,16,256]{0,2,1:T(8,128)(2,1)} %bitcast.5), calls=%async_computation | async-start | bytes 2097152 | tf_op jit(solution)/shard_map/all_to_all | solution.py:22
  228.0 6.8 %copy-start.2 = (bf16[1,128,512]{2,1,0:T(8,128)(2,1)S(1)}, bf16[1,128,512]{2,1,0:T(8,128)(2,1)}, u32[]{:S(2)}) copy-start(bf16[1,128,512]{2,1,0:T(8,128)(2,1)} %param.8) | copy-start | bytes 393220
  231.1 3.7 %copy-start = (bf16[1,4096,512]{2,1,0:T(8,128)(2,1)S(1)}, bf16[1,4096,512]{2,1,0:T(8,128)(2,1)}, u32[]{:S(2)}) copy-start(bf16[1,4096,512]{2,1,0:T(8,128)(2,1)} %all-gather.5.cloned.1.call-done) | copy-start | bytes 12582916
Sparse Core Ops, SparseCore 0:
  11.6 152.3 reduce-scatter.1
Sparse Core Ops, SparseCore 1:
  12.5 65.7 all-gather.6
  81.4 71.1 all-gather.4
where the time goes:
time: 246 us; the launch traced here: 245 us
  waiting for transfers between devices  144 us (59%)
  blocking collectives  62.1 us (25%)
  between operations  15.5 us (6%)
  starting transfers between devices  9.41 us (4%)
  matrix products  9.23 us (4%)
  local copies, waits for them, and re-layouts  3.52 us (1%)
    reduce_scatter x1, waiting for transfers between devices, on_device(): lax.psum_scatter(weight.astype(jnp.float32).astype(jnp.bfloat16), 'replic...  143 us
    all_gather x1, blocking collectives, on_device(): lax.all_gather(global_new.astype(jnp.bfloat16), 'replica', axis=0, tiled=...  62.1 us
    all_to_all x1, starting transfers between devices, on_device(): lax.all_to_all(inputs, 'fsdp', split_axis=1, concat_axis=0, tiled=True)  9.29 us
  transfers between devices with their start and end apart: 4, of which 1 were waited for; matrix products, arithmetic and copies ran while one was open for 3% of the time, Pallas kernels for 0%

commit v1 on v0

v1 whole, which is shorter than its diff:
```python
import jax
import jax.numpy as jnp
from jax import lax
from jax.experimental import pallas as pl
from jax.experimental.pallas import tpu as pltpu
from jax.sharding import PartitionSpec as P

MESH = pl.DeviceIdType.MESH
BF16, F32 = jnp.bfloat16, jnp.float32
SCALE = 1.0 / 4096**0.5
N_REPLICA = 32
NX, NZ = 4, 16
TOK, ROWS, KVW = 128, 256, 512


def kernel(
    tok, w, cot, glob, mom, anc,
    keys_o, gt_o, dw_o, mom_o, glob_o, syn_o,
    wbuf, tokv, tbuf, cbuf, acc, dwacc, gsend, grecv, sbuf, ybuf, zsum, rbuf, gma, res,
    ss_w, rs_w, ss_t, rs_t, ss_c, rs_c, ss_g, rs_g, ss_y, rs_y, ss_z, rs_z,
    ss_b, rs_b, ss_f, rs_f, ss_p, rs_p, ss_q, rs_q, loc,
):
    r, f = lax.axis_index("replica"), lax.axis_index("fsdp")
    z, yl = r // 2, r % 2
    x, yh, c = f // 4, (f // 2) % 2, f % 2
    xp, xm, x2 = (x + 1) % NX, (x + 3) % NX, (x + 2) % NX
    odd = (z + yl) % 2

    def at_x(other):
        return (r, other * 4 + yh * 2 + c)

    core = (r, x * 4 + yh * 2 + (1 - c))
    side = (r, x * 4 + (1 - yh) * 2 + c)
    cross = (r, x * 4 + (1 - yh) * 2 + (1 - c))
    pair = (z * 2 + (1 - yl), f)
    right, left, far = at_x(xp), at_x(xm), at_x(x2)

    def at_z(step):
        return (((z + step) % NZ) * 2 + yl, f)

    def remote(src, dst, send_sem, recv_sem, device):
        return pltpu.make_async_remote_copy(
            src_ref=src, dst_ref=dst, send_sem=send_sem, recv_sem=recv_sem,
            device_id=device, device_id_type=MESH,
        )

    def columns(xx, hh, cc):
        return pl.ds(pl.multiple_of((xx * 4 + hh * 2 + cc) * ROWS, ROWS), ROWS)

    xs_t = (x, xp, xm, x2)
    local = [
        pltpu.make_async_copy(w, wbuf.at[0], loc.at[0]),
        pltpu.make_async_copy(tok, tokv, loc.at[1]),
        pltpu.make_async_copy(cot, cbuf.at[pl.ds(0, TOK)], loc.at[2]),
        pltpu.make_async_copy(w.at[:, yl], sbuf, loc.at[3]),
        pltpu.make_async_copy(glob, gma.at[yl, 0], loc.at[4]),
        pltpu.make_async_copy(mom, gma.at[yl, 1], loc.at[5]),
        pltpu.make_async_copy(anc, gma.at[yl, 2], loc.at[6]),
    ] + [
        pltpu.make_async_copy(
            tok.at[:, columns(xs_t[i], yh, c)], tbuf.at[i, pl.ds(0, TOK)], loc.at[7 + i]
        )
        for i in range(4)
    ]
    for copy in local:
        copy.start()

    barrier = pltpu.get_barrier_semaphore()
    peers = [right, left, far, core, side, cross, pair] + [at_z(d) for d in range(1, NZ)]
    for peer in peers:
        pl.semaphore_signal(barrier, inc=1, device_id=peer, device_id_type=MESH)
    pl.semaphore_wait(barrier, len(peers))

    def half(ref, h):
        return ref.at[pl.ds(4 * h, 4)]

    sent = []

    def go(copy):
        copy.start()
        sent.append(copy)

    def w_send(src, slot, h, device):
        k = 2 * slot + h
        go(remote(src, half(wbuf.at[slot], h), ss_w.at[k], rs_w.at[k], device))

    def w_wait(slot, h):
        k = 2 * slot + h
        there = half(wbuf.at[slot], h)
        remote(there, there, ss_w.at[k], rs_w.at[k], core).wait_recv()

    def w_fwd(slot, h, to, device):
        w_send(half(wbuf.at[slot], h), to, h, device)

    go(remote(w.at[:, 1 - yl], ybuf, ss_y.at[0], rs_y.at[0], pair))
    w_send(half(w, 0), 1, 0, right)
    w_send(half(w, 1), 2, 1, left)
    w_send(half(w, 0), 4, 0, side)
    w_send(half(w, 0), 8, 0, core)
    w_send(half(w, 1), 8, 1, core)
    w_send(half(w, 1), 1, 1, right)
    w_send(half(w, 0), 2, 0, left)
    w_send(half(w, 1), 4, 1, side)

    def c_send(src, s, device):
        go(remote(src, cbuf.at[pl.ds(s * TOK, TOK)], ss_c.at[s], rs_c.at[s], device))

    def c_wait(s):
        there = cbuf.at[pl.ds(s * TOK, TOK)]
        remote(there, there, ss_c.at[s], rs_c.at[s], core).wait_recv()

    c_send(cot, 2, side)
    c_send(cot, 1, core)

    def t_send(i, s, hh, cc, device):
        k = 4 * i + s
        go(remote(
            tok.at[:, columns(xs_t[i], hh, cc)], tbuf.at[i, pl.ds(s * TOK, TOK)],
            ss_t.at[k], rs_t.at[k], device,
        ))

    def t_wait(i, s):
        there = tbuf.at[i, pl.ds(s * TOK, TOK)]
        remote(there, there, ss_t.at[4 * i + s], rs_t.at[4 * i + s], core).wait_recv()

    for i in (1, 2, 3, 0):
        t_send(i, 2, 1 - yh, c, side)
        t_send(i, 3, 1 - yh, 1 - c, cross)
        t_send(i, 1, yh, 1 - c, core)

    def p_copies():
        return [
            remote(src, gma.at[yl, n], ss_p.at[n], rs_p.at[n], pair)
            for n, src in enumerate((glob, mom, anc))
        ]

    @pl.when(odd == 1)
    def _():
        for copy in p_copies():
            copy.start()

    xs_w = (x, xm, xp, x2)

    def block(slot, first=False):
        cols = columns(
            xs_w[slot % 4],
            yh if slot % 8 < 4 else 1 - yh,
            c if slot < 8 else 1 - c,
        )
        weight = wbuf[slot].reshape(ROWS, KVW)
        part = jnp.dot(tokv[:, cols], weight, preferred_element_type=F32)
        if first:
            acc[...] = part
        else:
            acc[...] += part
        back = lax.dot_general(
            cbuf[0:TOK], weight, (((1,), (1,)), ((), ())), preferred_element_type=F32
        )
        gt_o[:, cols] = (back * SCALE).astype(BF16)

    def partial_sum(i):
        return lax.dot_general(
            tbuf[i], cbuf[...], (((0,), (0,)), ((), ())), preferred_element_type=F32
        )

    def g_copy(i):
        device = (None, right, left, far)[i]
        return remote(
            gsend.at[i - 1], grecv.at[i - 1], ss_g.at[i - 1], rs_g.at[i - 1], device
        )

    local[0].wait()
    local[1].wait()
    local[2].wait()
    block(0, first=True)
    w_wait(8, 0)
    w_wait(8, 1)
    block(8)

    local[3].wait()
    remote(ybuf, ybuf, ss_y.at[0], rs_y.at[0], pair).wait_recv()
    zsum[...] = (sbuf[...].astype(F32) + ybuf[...].astype(F32)).astype(BF16)

    def z_copy(j):
        step = 2 * j + odd
        return remote(
            zsum.at[((z + step) % NZ) // 2], rbuf.at[step], ss_z.at[j], rs_z.at[step], at_z(step)
        )

    for j in (4, 3, 5, 2, 6, 1, 7):
        z_copy(j).start()

    @pl.when(odd == 1)
    def _():
        z_copy(0).start()

    w_wait(1, 0)
    w_fwd(1, 0, 3, right)
    w_wait(2, 1)
    w_fwd(2, 1, 3, left)
    w_wait(4, 0)
    w_fwd(4, 0, 5, right)
    w_fwd(1, 0, 9, core)
    w_fwd(2, 1, 10, core)
    w_fwd(4, 0, 12, core)
    w_wait(4, 1)
    w_fwd(4, 1, 6, left)
    w_fwd(4, 1, 5, right)
    w_fwd(4, 0, 6, left)
    w_fwd(4, 1, 12, core)
    w_wait(1, 1)
    w_fwd(1, 1, 9, core)
    w_wait(2, 0)
    w_fwd(2, 0, 10, core)
    block(1)
    block(2)
    block(4)
    for slot in (9, 10, 12):
        w_wait(slot, 0)
        w_wait(slot, 1)
        block(slot)
    c_wait(2)
    c_send(cbuf.at[pl.ds(2 * TOK, TOK)], 3, core)
    w_wait(3, 0)
    w_fwd(3, 0, 11, core)
    w_wait(3, 1)
    w_fwd(3, 1, 11, core)
    block(3)
    w_wait(11, 0)
    w_wait(11, 1)
    block(11)

    def make_partial(i):
        local[7 + i].wait()
        for s in (1, 2, 3):
            t_wait(i, s)
        if i == 0:
            dwacc[...] = partial_sum(0)
        else:
            gsend[i - 1] = partial_sum(i).astype(BF16)
            go(g_copy(i))

    c_wait(1)
    c_wait(3)
    make_partial(1)

    for n in (4, 5, 6):
        local[n].wait()

    def syn_copy(d):
        return remote(syn_o.at[z], syn_o.at[z], ss_b.at[d], rs_b.at[d], at_z(d))

    def res_copies():
        return [
            remote(res.at[1 - yl, n], res.at[1 - yl, n], ss_q.at[n], rs_q.at[n], pair)
            for n in range(2)
        ]

    @pl.when(odd == 0)
    def _():
        rbuf[0] = zsum[z // 2]
        for copy in p_copies():
            copy.wait_recv()
        for d in range(1, NZ):
            remote(rbuf.at[d], rbuf.at[d], ss_z.at[0], rs_z.at[d], pair).wait_recv()
        total = rbuf[0].astype(F32)
        for d in range(1, NZ):
            total = total + rbuf[d].astype(F32)
        fresh = []
        for owner in range(2):
            g, m, a = gma[owner, 0], gma[owner, 1], gma[owner, 2]
            pseudo = g - total[8 * owner : 8 * owner + 8] / N_REPLICA
            push = pseudo + 0.1 * (g - a)
            m_new = 0.9 * m + push
            g_new = g - 0.7 * (push + 0.9 * m_new)
            res[owner, 0] = m_new
            res[owner, 1] = g_new
            fresh.append(g_new)
        syn_o[z] = jnp.concatenate(fresh, axis=0).astype(BF16)
        for d in (8, 7, 9, 6, 10, 5, 11, 4, 12, 3, 13, 2, 14, 1, 15):
            syn_copy(d).start()
        for copy in res_copies():
            copy.start()

    w_wait(5, 0)
    w_fwd(5, 0, 7, right)
    w_wait(6, 1)
    w_fwd(6, 1, 7, left)
    w_fwd(5, 0, 13, core)
    w_fwd(6, 1, 14, core)
    make_partial(2)
    w_wait(5, 1)
    w_fwd(5, 1, 13, core)
    w_wait(6, 0)
    w_fwd(6, 0, 14, core)
    block(5)
    block(6)
    make_partial(3)
    for slot in (13, 14):
        w_wait(slot, 0)
        w_wait(slot, 1)
        block(slot)
    w_wait(7, 0)
    w_fwd(7, 0, 15, core)
    w_wait(7, 1)
    w_fwd(7, 1, 15, core)
    block(7)
    make_partial(0)
    w_wait(15, 0)
    w_wait(15, 1)
    block(15)
    keys_o[...] = (acc[...] * SCALE).astype(BF16)

    def hand(j):
        place = (z - 2 * j - odd + NZ) % NZ
        return remote(syn_o.at[place], syn_o.at[place], ss_f.at[j], rs_f.at[j], pair)

    def taken(j):
        place = (z - 2 * j - (1 - odd) + NZ) % NZ
        return remote(syn_o.at[place], syn_o.at[place], ss_f.at[j], rs_f.at[j], pair)

    def arrive(j):
        step = 2 * j + odd
        place = (z - step + NZ) % NZ
        remote(syn_o.at[place], syn_o.at[place], ss_b.at[0], rs_b.at[step], pair).wait_recv()

    @pl.when(odd == 1)
    def _():
        arrive(0)

    hand(0).start()
    for j in (1, 7, 2, 6, 3, 5, 4):
        arrive(j)
        hand(j).start()

    for i in (1, 2, 3):
        g_copy(i).wait_recv()
    total = dwacc[...]
    for n in range(3):
        total = total + grecv[n].astype(F32)
    dw_o[...] = (total * SCALE).astype(BF16)

    @pl.when(odd == 1)
    def _():
        for n in range(2):
            remote(res.at[yl, n], res.at[yl, n], ss_q.at[n], rs_q.at[n], pair).wait_recv()

    mom_o[...] = res[yl, 0]
    glob_o[...] = res[yl, 1]
    for j in range(8):
        taken(j).wait_recv()

    for copy in sent:
        copy.wait_send()
    for j in range(1, 8):
        z_copy(j).wait_send()
    for j in range(8):
        hand(j).wait_send()

    @pl.when(odd == 1)
    def _():
        z_copy(0).wait_send()
        for copy in p_copies():
            copy.wait_send()

    @pl.when(odd == 0)
    def _():
        for d in range(1, NZ):
            syn_copy(d).wait_send()
        for copy in res_copies():
            copy.wait_send()


def on_device(tokens, local_weight, key_cot, global_weight, momentum, anchor):
    dma, vmem = pltpu.SemaphoreType.DMA, pltpu.VMEM
    scratch = [
        vmem((16, 8, 2, 16, KVW), BF16),
        vmem((TOK, 4096), BF16),
        vmem((4, 4 * TOK, ROWS), BF16),
        vmem((4 * TOK, KVW), BF16),
        vmem((TOK, KVW), F32),
        vmem((ROWS, KVW), F32),
        vmem((3, ROWS, KVW), BF16),
        vmem((3, ROWS, KVW), BF16),
        vmem((8, 16, KVW), BF16),
        vmem((8, 16, KVW), BF16),
        vmem((8, 16, KVW), BF16),
        vmem((16, 16, KVW), BF16),
        vmem((2, 3, 8, KVW), F32),
        vmem((2, 2, 8, KVW), F32),
        dma((32,)), dma((32,)),
        dma((16,)), dma((16,)),
        dma((4,)), dma((4,)),
        dma((3,)), dma((3,)),
        dma((1,)), dma((1,)),
        dma((8,)), dma((16,)),
        dma((16,)), dma((16,)),
        dma((8,)), dma((8,)),
        dma((3,)), dma((3,)),
        dma((2,)), dma((2,)),
        dma((11,)),
    ]
    hbm, in_vmem = pl.BlockSpec(memory_space=pl.ANY), pl.BlockSpec(memory_space=vmem)
    keys, gt, dw, mom, glob, syn = pl.pallas_call(
        kernel,
        out_shape=(
            jax.ShapeDtypeStruct((TOK, KVW), BF16),
            jax.ShapeDtypeStruct((TOK, 4096), BF16),
            jax.ShapeDtypeStruct((ROWS, KVW), BF16),
            jax.ShapeDtypeStruct((8, KVW), F32),
            jax.ShapeDtypeStruct((8, KVW), F32),
            jax.ShapeDtypeStruct((16, 16, KVW), BF16),
        ),
        in_specs=[hbm] * 6,
        out_specs=[in_vmem] * 6,
        scratch_shapes=scratch,
        compiler_params=pltpu.CompilerParams(
            collective_id=0, has_side_effects=True, vmem_limit_bytes=40 * 2**20
        ),
        cost_estimate=pl.CostEstimate(
            flops=6 * 128 * 4096 * 512, bytes_accessed=4 * 2**20, transcendentals=0
        ),
        name="step",
    )(
        tokens[0],
        local_weight.reshape(8, 2, 16, KVW),
        key_cot[0],
        global_weight,
        momentum,
        anchor,
    )
    return keys[None], gt[None], dw[None], mom, glob, syn.reshape(ROWS, KVW)


def solution(mesh):
    in_specs = (
        P("replica", "fsdp", None),
        P("replica", "fsdp", None),
        P("replica", "fsdp", None),
        P(("fsdp", "replica"), None),
        P(("fsdp", "replica"), None),
        P(("fsdp", "replica"), None),
    )
    out_specs = (
        P("replica", "fsdp", None),
        P("replica", "fsdp", None),
        P("replica", "fsdp", None),
        P(("fsdp", "replica"), None),
        P(("fsdp", "replica"), None),
        P("fsdp", None),
    )
    return jax.shard_map(
        on_device, mesh=mesh, in_specs=in_specs, out_specs=out_specs, check_vma=False
    )
```

time: 246 us -> 69.4 us (0.28)
  the two profiles are of different devices: /device:TPU:16 before, /device:TPU:2 now
where the time goes in v1:
time: 69.4 us; the launch traced here: 69 us
  Pallas kernels  58.9 us (85%)
  local copies, waits for them, and re-layouts  9.46 us (14%)
    pallas_call x1, Pallas kernels, on_device(): pl.pallas_call(kernel, out_shape=(jax.ShapeDtypeStruct((TOK, KVW), BF16),...  58.9 us
    unnamed x18, local copies, waits for them, and re-layouts  9.46 us

profile of v1, /device:TPU:2, one launch (start us, length us, event | category | flops | bytes accessed | tf_op | source)
XLA Modules:
  0.0 69.0 jit_solution(3403556999383880756)
XLA Ops:
  0.6 0.0 copy-start
  0.6 1.2 %copy-done = bf16[1,128,4096]{2,1,0:T(8,128)(2,1)S(1)} copy-done((bf16[1,128,4096]{2,1,0:T(8,128)(2,1)S(1)}, bf16[1,128,4096]{2,1,0:T(8,128)(2,1)}, u32[]{:S(2)}) %copy-start) | copy-done | bytes 1048600
  1.9 0.0 copy-start.1
  1.9 0.9 %copy-done.1 = bf16[1,256,512]{2,1,0:T(8,128)(2,1)S(1)} copy-done((bf16[1,256,512]{2,1,0:T(8,128)(2,1)S(1)}, bf16[1,256,512]{2,1,0:T(8,128)(2,1)}, u32[]{:S(2)}) %copy-start.1) | copy-done | bytes 262168
  2.8 0.0 copy-start.2
  2.8 0.9 %copy-done.2 = bf16[1,128,512]{2,1,0:T(8,128)(2,1)S(1)} copy-done((bf16[1,128,512]{2,1,0:T(8,128)(2,1)S(1)}, bf16[1,128,512]{2,1,0:T(8,128)(2,1)}, u32[]{:S(2)}) %copy-start.2) | copy-done | bytes 131096
  3.7 0.0 copy-start.3
  3.7 0.7 %copy-done.3 = f32[8,512]{1,0:T(8,128)S(1)} copy-done((f32[8,512]{1,0:T(8,128)S(1)}, f32[8,512]{1,0:T(8,128)}, u32[]{:S(2)}) %copy-start.3) | copy-done | bytes 16408
  4.4 0.0 copy-start.4
  4.4 0.7 %copy-done.4 = f32[8,512]{1,0:T(8,128)S(1)} copy-done((f32[8,512]{1,0:T(8,128)S(1)}, f32[8,512]{1,0:T(8,128)}, u32[]{:S(2)}) %copy-start.4) | copy-done | bytes 16408
  5.2 0.0 copy-start.5
  5.2 0.7 %copy-done.5 = f32[8,512]{1,0:T(8,128)S(1)} copy-done((f32[8,512]{1,0:T(8,128)S(1)}, f32[8,512]{1,0:T(8,128)}, u32[]{:S(2)}) %copy-start.5) | copy-done | bytes 16408
  5.9 58.9 %step.1 = (bf16[128,512]{1,0:T(8,128)(2,1)S(1)}, bf16[128,4096]{1,0:T(8,128)(2,1)S(1)}, bf16[256,512]{1,0:T(8,128)(2,1)S(1)}, f32[8,512]{1,0:T(8,128)S(1)}, f32[...) custom-call(bf16[128,4096]{1,0:T(8,128)(2,1)S(1)} %bitcast.11, bf16[8,2,16,512]{3,2,1,0:T(8,128)(2,1)S(1)} %bitcast.12, ...), custom_call_target="tpu_custom_call" | custom-call | flops 1610612736 | bytes 4194304 | tf_op jit(solution)/shard_map/step/pallas_call | solution.py:404
  64.8 0.7 copy.18
  65.4 1.0 %copy.19 = bf16[1,128,4096]{2,1,0:T(8,128)(2,1)} copy(bf16[1,128,4096]{2,1,0:T(8,128)(2,1)S(1)} %bitcast.7) | data formatting | bytes 2097152
  66.4 0.7 %copy.20 = bf16[1,256,512]{2,1,0:T(8,128)(2,1)} copy(bf16[1,256,512]{2,1,0:T(8,128)(2,1)S(1)} %bitcast.9) | data formatting | bytes 524288
  67.1 0.6 copy.21
  67.7 0.6 copy.22
  68.3 0.7 %copy.23 = bf16[256,512]{1,0:T(8,128)(2,1)} copy(bf16[256,512]{1,0:T(8,128)(2,1)S(1)} %bitcast.8) | data formatting | bytes 524288
Async XLA Ops:
  0.6 1.2 %copy-start = (bf16[1,128,4096]{2,1,0:T(8,128)(2,1)S(1)}, bf16[1,128,4096]{2,1,0:T(8,128)(2,1)}, u32[]{:S(2)}) copy-start(bf16[1,128,4096]{2,1,0:T(8,128)(2,1)} %param.6) | copy-start | bytes 3145732
  1.9 0.9 %copy-start.1 = (bf16[1,256,512]{2,1,0:T(8,128)(2,1)S(1)}, bf16[1,256,512]{2,1,0:T(8,128)(2,1)}, u32[]{:S(2)}) copy-start(bf16[1,256,512]{2,1,0:T(8,128)(2,1)} %param.7) | copy-start | bytes 786436
  2.8 0.9 %copy-start.2 = (bf16[1,128,512]{2,1,0:T(8,128)(2,1)S(1)}, bf16[1,128,512]{2,1,0:T(8,128)(2,1)}, u32[]{:S(2)}) copy-start(bf16[1,128,512]{2,1,0:T(8,128)(2,1)} %param.8) | copy-start | bytes 393220
  3.7 0.7 %copy-start.3 = (f32[8,512]{1,0:T(8,128)S(1)}, f32[8,512]{1,0:T(8,128)}, u32[]{:S(2)}) copy-start(f32[8,512]{1,0:T(8,128)} %glob.1) | copy-start | bytes 49156
  4.4 0.7 %copy-start.4 = (f32[8,512]{1,0:T(8,128)S(1)}, f32[8,512]{1,0:T(8,128)}, u32[]{:S(2)}) copy-start(f32[8,512]{1,0:T(8,128)} %mom.1) | copy-start | bytes 49156
  5.2 0.7 %copy-start.5 = (f32[8,512]{1,0:T(8,128)S(1)}, f32[8,512]{1,0:T(8,128)}, u32[]{:S(2)}) copy-start(f32[8,512]{1,0:T(8,128)} %anc.1) | copy-start | bytes 49156

commit v2 on v1

--- a/solution.py
+++ b/solution.py
@@ -18,7 +18,7 @@
     keys_o, gt_o, dw_o, mom_o, glob_o, syn_o,
     wbuf, tokv, tbuf, cbuf, acc, dwacc, gsend, grecv, sbuf, ybuf, zsum, rbuf, gma, res,
     ss_w, rs_w, ss_t, rs_t, ss_c, rs_c, ss_g, rs_g, ss_y, rs_y, ss_z, rs_z,
-    ss_b, rs_b, ss_f, rs_f, ss_p, rs_p, ss_q, rs_q, loc,
+    ss_b, rs_b, ss_f, rs_f, ss_p, rs_p, ss_q, rs_q, loc, here,
 ):
     r, f = lax.axis_index("replica"), lax.axis_index("fsdp")
     z, yl = r // 2, r % 2
@@ -66,10 +66,18 @@
         copy.start()
 
     barrier = pltpu.get_barrier_semaphore()
-    peers = [right, left, far, core, side, cross, pair] + [at_z(d) for d in range(1, NZ)]
+    peers = [right, left, far, core, side, cross, pair]
     for peer in peers:
         pl.semaphore_signal(barrier, inc=1, device_id=peer, device_id_type=MESH)
-    pl.semaphore_wait(barrier, len(peers))
+    late = z >= NZ // 2
+    for d in range(1, NZ):
+        there = (z + d) % NZ
+
+        @pl.when((there > z) | (late & (there >= NZ // 2)))
+        def _():
+            pl.semaphore_signal(barrier, inc=1, device_id=at_z(d), device_id_type=MESH)
+
+    pl.semaphore_wait(barrier, len(peers) + jnp.where(late, NZ - 1, z))
 
     def half(ref, h):
         return ref.at[pl.ds(4 * h, 4)]
@@ -128,6 +136,13 @@
         t_send(i, 3, 1 - yh, 1 - c, cross)
         t_send(i, 1, yh, 1 - c, core)
 
+    for d in range(1, NZ):
+        there = (z + d) % NZ
+
+        @pl.when((there < z) & (there < NZ // 2))
+        def _():
+            pl.semaphore_signal(here, inc=1, device_id=at_z(d), device_id_type=MESH)
+
     def p_copies():
         return [
             remote(src, gma.at[yl, n], ss_p.at[n], rs_p.at[n], pair)
@@ -187,12 +202,20 @@
             zsum.at[((z + step) % NZ) // 2], rbuf.at[step], ss_z.at[j], rs_z.at[step], at_z(step)
         )
 
-    for j in (4, 3, 5, 2, 6, 1, 7):
-        z_copy(j).start()
-
-    @pl.when(odd == 1)
-    def _():
-        z_copy(0).start()
+    def z_sends():
+        for j in (4, 3, 5, 2, 6, 1, 7):
+            z_copy(j).start()
+
+        @pl.when(odd == 1)
+        def _():
+            z_copy(0).start()
+
+    @pl.when(late)
+    def _():
+        z_sends()
+
+    middle = (z >= NZ // 4) & (z < NZ // 2)
+    early = z < NZ // 4
 
     w_wait(1, 0)
     w_fwd(1, 0, 3, right)
@@ -219,6 +242,12 @@
         w_wait(slot, 0)
         w_wait(slot, 1)
         block(slot)
+
+    @pl.when(middle)
+    def _():
+        pl.semaphore_wait(here, NZ - 1 - z)
+        z_sends()
+
     c_wait(2)
     c_send(cbuf.at[pl.ds(2 * TOK, TOK)], 3, core)
     w_wait(3, 0)
@@ -244,6 +273,11 @@
     c_wait(3)
     make_partial(1)
 
+    @pl.when(early)
+    def _():
+        pl.semaphore_wait(here, NZ - 1 - z)
+        z_sends()
+
     for n in (4, 5, 6):
         local[n].wait()
 
@@ -256,8 +290,7 @@
             for n in range(2)
         ]
 
-    @pl.when(odd == 0)
-    def _():
+    def update():
         rbuf[0] = zsum[z // 2]
         for copy in p_copies():
             copy.wait_recv()
@@ -282,6 +315,10 @@
         for copy in res_copies():
             copy.start()
 
+    @pl.when((odd == 0) & late)
+    def _():
+        update()
+
     w_wait(5, 0)
     w_fwd(5, 0, 7, right)
     w_wait(6, 1)
@@ -296,6 +333,11 @@
     block(5)
     block(6)
     make_partial(3)
+
+    @pl.when((odd == 0) & middle)
+    def _():
+        update()
+
     for slot in (13, 14):
         w_wait(slot, 0)
         w_wait(slot, 1)
@@ -311,27 +353,9 @@
     block(15)
     keys_o[...] = (acc[...] * SCALE).astype(BF16)
 
-    def hand(j):
-        place = (z - 2 * j - odd + NZ) % NZ
-        return remote(syn_o.at[place], syn_o.at[place], ss_f.at[j], rs_f.at[j], pair)
-
-    def taken(j):
-        place = (z - 2 * j - (1 - odd) + NZ) % NZ
-        return remote(syn_o.at[place], syn_o.at[place], ss_f.at[j], rs_f.at[j], pair)
-
-    def arrive(j):
-        step = 2 * j + odd
-        place = (z - step + NZ) % NZ
-        remote(syn_o.at[place], syn_o.at[place], ss_b.at[0], rs_b.at[step], pair).wait_recv()
-
-    @pl.when(odd == 1)
-    def _():
-        arrive(0)
-
-    hand(0).start()
-    for j in (1, 7, 2, 6, 3, 5, 4):
-        arrive(j)
-        hand(j).start()
+    @pl.when((odd == 0) & early)
+    def _():
+        update()
 
     for i in (1, 2, 3):
         g_copy(i).wait_recv()
@@ -340,6 +364,28 @@
         total = total + grecv[n].astype(F32)
     dw_o[...] = (total * SCALE).astype(BF16)
 
+    def hand(j):
+        place = (z - 2 * j - odd + NZ) % NZ
+        return remote(syn_o.at[place], syn_o.at[place], ss_f.at[j], rs_f.at[j], pair)
+
+    def taken(j):
+        place = (z - 2 * j - (1 - odd) + NZ) % NZ
+        return remote(syn_o.at[place], syn_o.at[place], ss_f.at[j], rs_f.at[j], pair)
+
+    def arrive(j):
+        step = 2 * j + odd
+        place = (z - step + NZ) % NZ
+        remote(syn_o.at[place], syn_o.at[place], ss_b.at[0], rs_b.at[step], pair).wait_recv()
+
+    @pl.when(odd == 1)
+    def _():
+        arrive(0)
+
+    hand(0).start()
+    for j in (1, 7, 2, 6, 3, 5, 4):
+        arrive(j)
+        hand(j).start()
+
     @pl.when(odd == 1)
     def _():
         for n in range(2):
@@ -369,6 +415,26 @@
             syn_copy(d).wait_send()
         for copy in res_copies():
             copy.wait_send()
+
+
+def write_out(*refs):
+    came, go, held, sem = refs[:6], refs[6:12], refs[12:18], refs[18]
+    copies = []
+    for n in (1, 2, 5, 0, 3, 4):
+        rows = came[n].shape[0] // 2 if n == 1 else came[n].shape[0]
+        for at in range(0, came[n].shape[0], rows):
+            k, part = len(copies), pl.ds(at, rows)
+            copies.append((
+                pltpu.make_async_copy(came[n].at[part], held[n].at[part], sem.at[0, k]),
+                pltpu.make_async_copy(held[n].at[part], go[n].at[part], sem.at[1, k]),
+            ))
+    for copy, _ in copies:
+        copy.start()
+    for copy, out in copies:
+        copy.wait()
+        out.start()
+    for _, out in copies:
+        out.wait()
 
 
 def on_device(tokens, local_weight, key_cot, global_weight, momentum, anchor):
@@ -399,9 +465,10 @@
         dma((3,)), dma((3,)),
         dma((2,)), dma((2,)),
         dma((11,)),
+        pltpu.SemaphoreType.REGULAR,
     ]
     hbm, in_vmem = pl.BlockSpec(memory_space=pl.ANY), pl.BlockSpec(memory_space=vmem)
-    keys, gt, dw, mom, glob, syn = pl.pallas_call(
+    made = pl.pallas_call(
         kernel,
         out_shape=(
             jax.ShapeDtypeStruct((TOK, KVW), BF16),
@@ -415,7 +482,7 @@
         out_specs=[in_vmem] * 6,
         scratch_shapes=scratch,
         compiler_params=pltpu.CompilerParams(
-            collective_id=0, has_side_effects=True, vmem_limit_bytes=40 * 2**20
+            collective_id=0, has_side_effects=True, vmem_limit_bytes=60 * 2**20
         ),
         cost_estimate=pl.CostEstimate(
             flops=6 * 128 * 4096 * 512, bytes_accessed=4 * 2**20, transcendentals=0
@@ -429,6 +496,15 @@
         momentum,
         anchor,
     )
+    keys, gt, dw, mom, glob, syn = pl.pallas_call(
+        write_out,
+        out_shape=tuple(jax.ShapeDtypeStruct(m.shape, m.dtype) for m in made),
+        in_specs=[hbm] * 6,
+        out_specs=[hbm] * 6,
+        scratch_shapes=[vmem(m.shape, m.dtype) for m in made] + [dma((2, 7))],
+        compiler_params=pltpu.CompilerParams(vmem_limit_bytes=60 * 2**20),
+        name="write_out",
+    )(*made)
     return keys[None], gt[None], dw[None], mom, glob, syn.reshape(ROWS, KVW)
 
 

time: 69.4 us -> 57.6 us (0.83)
  the two profiles are of different devices: /device:TPU:2 before, /device:TPU:498 now
where the time goes in v2:
time: 57.6 us; the launch traced here: 57.4 us
  Pallas kernels  56.8 us (99%)
  between operations  0.64 us (1%)
    pallas_call x1, Pallas kernels, on_device(): pl.pallas_call(kernel, out_shape=(jax.ShapeDtypeStruct((TOK, KVW), BF16),...  54.4 us
    pallas_call x1, Pallas kernels, on_device(): pl.pallas_call(write_out, out_shape=tuple((jax.ShapeDtypeStruct(m.shape,...  2.34 us

profile of v2, /device:TPU:498, one launch (start us, length us, event | category | flops | bytes accessed | tf_op | source)
XLA Modules:
  0.0 57.4 jit_solution(13715927811857065323)
XLA Ops:
  0.6 54.4 %step.1 = (bf16[128,512]{1,0:T(8,128)(2,1)}, bf16[128,4096]{1,0:T(8,128)(2,1)}, bf16[256,512]{1,0:T(8,128)(2,1)}, f32[8,512]{1,0:T(8,128)}, f32[8,512]{1,0:T(8,128)}, /*index=5*/bf16[16,16,512]{2,1,0:T(8,128)(2,1)}) custom-call(bf16[128,4096]{1,0:T(8,128)(2,1)} %bitcast.7, bf16[8,2,16,512]{3,2,1,0:T(8,128)(2,1)} %bitcast.9, bf16[128,512]{1,0:T(8,128)(2,1)} %bitcast.12, ...), custom_call_target="tpu_custom_call" | custom-call | flops 1610612736 | bytes 4194304 | tf_op jit(solution)/shard_map/step/pallas_call | solution.py:471
  55.1 2.3 %write_out.1 = (bf16[128,512]{1,0:T(8,128)(2,1)}, bf16[128,4096]{1,0:T(8,128)(2,1)}, bf16[256,512]{1,0:T(8,128)(2,1)}, f32[8,512]{1,0:T(8,128)}, f32[8,512]{1,0:T(8,128)}, /*index=5*/bf16[16,16,512]{2,1,0:T(8,128)(2,1)}) custom-call(bf16[128,512]{1,0:T(8,128)(2,1)} %get-tuple-element.18.refs_0_, bf16[128,4096]{1,0:T(8,128)(2,1)} %get-tuple-element.19.refs_1_, ...), custom_call_target="tpu_custom_call" | custom-call | tf_op jit(solution)/shard_map/write_out/pallas_call | solution.py:499

commit v3 on v2

--- a/solution.py
+++ b/solution.py
@@ -70,14 +70,21 @@
     for peer in peers:
         pl.semaphore_signal(barrier, inc=1, device_id=peer, device_id_type=MESH)
     late = z >= NZ // 2
+
+    def rank(zz):
+        return jnp.where(zz < NZ // 2, zz, jnp.where(zz < 3 * NZ // 4, NZ, NZ - 1))
+
+    mine = rank(z)
     for d in range(1, NZ):
-        there = (z + d) % NZ
-
-        @pl.when((there > z) | (late & (there >= NZ // 2)))
+
+        @pl.when(rank((z + d) % NZ) >= mine)
         def _():
             pl.semaphore_signal(barrier, inc=1, device_id=at_z(d), device_id_type=MESH)
 
-    pl.semaphore_wait(barrier, len(peers) + jnp.where(late, NZ - 1, z))
+    last = z // (NZ // 4) == 2
+    above = jnp.where(late, jnp.where(last, 0, NZ // 4), NZ - 1 - z)
+    below = jnp.where(late, jnp.where(last, NZ - 1, 3 * NZ // 4 - 1), z)
+    pl.semaphore_wait(barrier, len(peers) + below)
 
     def half(ref, h):
         return ref.at[pl.ds(4 * h, 4)]
@@ -101,6 +108,18 @@
         w_send(half(wbuf.at[slot], h), to, h, device)
 
     go(remote(w.at[:, 1 - yl], ybuf, ss_y.at[0], rs_y.at[0], pair))
+
+    def p_copies():
+        return [
+            remote(src, gma.at[yl, n], ss_p.at[n], rs_p.at[n], pair)
+            for n, src in enumerate((glob, mom, anc))
+        ]
+
+    @pl.when(odd == 1)
+    def _():
+        for copy in p_copies():
+            copy.start()
+
     w_send(half(w, 0), 1, 0, right)
     w_send(half(w, 1), 2, 1, left)
     w_send(half(w, 0), 4, 0, side)
@@ -137,22 +156,10 @@
         t_send(i, 1, yh, 1 - c, core)
 
     for d in range(1, NZ):
-        there = (z + d) % NZ
-
-        @pl.when((there < z) & (there < NZ // 2))
+
+        @pl.when(rank((z + d) % NZ) < mine)
         def _():
             pl.semaphore_signal(here, inc=1, device_id=at_z(d), device_id_type=MESH)
-
-    def p_copies():
-        return [
-            remote(src, gma.at[yl, n], ss_p.at[n], rs_p.at[n], pair)
-            for n, src in enumerate((glob, mom, anc))
-        ]
-
-    @pl.when(odd == 1)
-    def _():
-        for copy in p_copies():
-            copy.start()
 
     xs_w = (x, xm, xp, x2)
 
@@ -210,17 +217,22 @@
         def _():
             z_copy(0).start()
 
-    @pl.when(late)
+    @pl.when(last)
     def _():
         z_sends()
 
-    middle = (z >= NZ // 4) & (z < NZ // 2)
     early = z < NZ // 4
 
     w_wait(1, 0)
     w_fwd(1, 0, 3, right)
     w_wait(2, 1)
     w_fwd(2, 1, 3, left)
+
+    @pl.when(jnp.logical_not(early | last))
+    def _():
+        pl.semaphore_wait(here, above)
+        z_sends()
+
     w_wait(4, 0)
     w_fwd(4, 0, 5, right)
     w_fwd(1, 0, 9, core)
@@ -231,6 +243,12 @@
     w_fwd(4, 1, 5, right)
     w_fwd(4, 0, 6, left)
     w_fwd(4, 1, 12, core)
+
+    @pl.when(early)
+    def _():
+        pl.semaphore_wait(here, above)
+        z_sends()
+
     w_wait(1, 1)
     w_fwd(1, 1, 9, core)
     w_wait(2, 0)
@@ -242,12 +260,6 @@
         w_wait(slot, 0)
         w_wait(slot, 1)
         block(slot)
-
-    @pl.when(middle)
-    def _():
-        pl.semaphore_wait(here, NZ - 1 - z)
-        z_sends()
-
     c_wait(2)
     c_send(cbuf.at[pl.ds(2 * TOK, TOK)], 3, core)
     w_wait(3, 0)
@@ -272,11 +284,6 @@
     c_wait(1)
     c_wait(3)
     make_partial(1)
-
-    @pl.when(early)
-    def _():
-        pl.semaphore_wait(here, NZ - 1 - z)
-        z_sends()
 
     for n in (4, 5, 6):
         local[n].wait()
@@ -334,7 +341,7 @@
     block(6)
     make_partial(3)
 
-    @pl.when((odd == 0) & middle)
+    @pl.when((odd == 0) & jnp.logical_not(late))
     def _():
         update()
 
@@ -353,9 +360,27 @@
     block(15)
     keys_o[...] = (acc[...] * SCALE).astype(BF16)
 
-    @pl.when((odd == 0) & early)
-    def _():
-        update()
+    def hand(j):
+        place = (z - 2 * j - odd + NZ) % NZ
+        return remote(syn_o.at[place], syn_o.at[place], ss_f.at[j], rs_f.at[j], pair)
+
+    def taken(j):
+        place = (z - 2 * j - (1 - odd) + NZ) % NZ
+        return remote(syn_o.at[place], syn_o.at[place], ss_f.at[j], rs_f.at[j], pair)
+
+    def arrive(j):
+        step = 2 * j + odd
+        place = (z - step + NZ) % NZ
+        remote(syn_o.at[place], syn_o.at[place], ss_b.at[0], rs_b.at[step], pair).wait_recv()
+
+    @pl.when(odd == 1)
+    def _():
+        arrive(0)
+
+    hand(0).start()
+    for j in (1, 7, 2, 6, 3, 5, 4):
+        arrive(j)
+        hand(j).start()
 
     for i in (1, 2, 3):
         g_copy(i).wait_recv()
@@ -363,28 +388,6 @@
     for n in range(3):
         total = total + grecv[n].astype(F32)
     dw_o[...] = (total * SCALE).astype(BF16)
-
-    def hand(j):
-        place = (z - 2 * j - odd + NZ) % NZ
-        return remote(syn_o.at[place], syn_o.at[place], ss_f.at[j], rs_f.at[j], pair)
-
-    def taken(j):
-        place = (z - 2 * j - (1 - odd) + NZ) % NZ
-        return remote(syn_o.at[place], syn_o.at[place], ss_f.at[j], rs_f.at[j], pair)
-
-    def arrive(j):
-        step = 2 * j + odd
-        place = (z - step + NZ) % NZ
-        remote(syn_o.at[place], syn_o.at[place], ss_b.at[0], rs_b.at[step], pair).wait_recv()
-
-    @pl.when(odd == 1)
-    def _():
-        arrive(0)
-
-    hand(0).start()
-    for j in (1, 7, 2, 6, 3, 5, 4):
-        arrive(j)
-        hand(j).start()
 
     @pl.when(odd == 1)
     def _():

time: 57.6 us -> 52 us (0.903)
  the two profiles are of different devices: /device:TPU:498 before, /device:TPU:1 now
where the time goes in v3:
time: 52 us; the launch traced here: 51.8 us
  Pallas kernels  51.2 us (98%)
  between operations  0.64 us (1%)
    pallas_call x1, Pallas kernels, on_device(): pl.pallas_call(kernel, out_shape=(jax.ShapeDtypeStruct((TOK, KVW), BF16),...  48.8 us
    pallas_call x1, Pallas kernels, on_device(): pl.pallas_call(write_out, out_shape=tuple((jax.ShapeDtypeStruct(m.shape,...  2.34 us

profile of v3, /device:TPU:1, one launch (start us, length us, event | category | flops | bytes accessed | tf_op | source)
XLA Modules:
  0.0 51.8 jit_solution(14144435663253941987)
XLA Ops:
  0.6 48.8 %step.1 = (bf16[128,512]{1,0:T(8,128)(2,1)}, bf16[128,4096]{1,0:T(8,128)(2,1)}, bf16[256,512]{1,0:T(8,128)(2,1)}, f32[8,512]{1,0:T(8,128)}, f32[8,512]{1,0:T(8,128)}, /*index=5*/bf16[16,16,512]{2,1,0:T(8,128)(2,1)}) custom-call(bf16[128,4096]{1,0:T(8,128)(2,1)} %bitcast.7, bf16[8,2,16,512]{3,2,1,0:T(8,128)(2,1)} %bitcast.9, bf16[128,512]{1,0:T(8,128)(2,1)} %bitcast.12, ...), custom_call_target="tpu_custom_call" | custom-call | flops 1610612736 | bytes 4194304 | tf_op jit(solution)/shard_map/step/pallas_call | solution.py:474
  49.5 2.3 %write_out.1 = (bf16[128,512]{1,0:T(8,128)(2,1)}, bf16[128,4096]{1,0:T(8,128)(2,1)}, bf16[256,512]{1,0:T(8,128)(2,1)}, f32[8,512]{1,0:T(8,128)}, f32[8,512]{1,0:T(8,128)}, /*index=5*/bf16[16,16,512]{2,1,0:T(8,128)(2,1)}) custom-call(bf16[128,512]{1,0:T(8,128)(2,1)} %get-tuple-element.18.refs_0_, bf16[128,4096]{1,0:T(8,128)(2,1)} %get-tuple-element.19.refs_1_, ...), custom_call_target="tpu_custom_call" | custom-call | tf_op jit(solution)/shard_map/write_out/pallas_call | solution.py:502

commit v4 on v3

--- a/solution.py
+++ b/solution.py
@@ -15,10 +15,11 @@
 
 def kernel(
     tok, w, cot, glob, mom, anc,
+    keys_h, gt_h, dw_h, mom_h, glob_h, syn_h,
     keys_o, gt_o, dw_o, mom_o, glob_o, syn_o,
     wbuf, tokv, tbuf, cbuf, acc, dwacc, gsend, grecv, sbuf, ybuf, zsum, rbuf, gma, res,
     ss_w, rs_w, ss_t, rs_t, ss_c, rs_c, ss_g, rs_g, ss_y, rs_y, ss_z, rs_z,
-    ss_b, rs_b, ss_f, rs_f, ss_p, rs_p, ss_q, rs_q, loc, here,
+    ss_b, rs_b, ss_f, rs_f, ss_p, rs_p, ss_q, rs_q, loc, here, out_sem,
 ):
     r, f = lax.axis_index("replica"), lax.axis_index("fsdp")
     z, yl = r // 2, r % 2
@@ -85,6 +86,11 @@
     above = jnp.where(late, jnp.where(last, 0, NZ // 4), NZ - 1 - z)
     below = jnp.where(late, jnp.where(last, NZ - 1, 3 * NZ // 4 - 1), z)
     pl.semaphore_wait(barrier, len(peers) + below)
+    for d in range(1, NZ):
+
+        @pl.when(rank((z + d) % NZ) < mine)
+        def _():
+            pl.semaphore_signal(here, inc=1, device_id=at_z(d), device_id_type=MESH)
 
     def half(ref, h):
         return ref.at[pl.ds(4 * h, 4)]
@@ -155,12 +161,6 @@
         t_send(i, 3, 1 - yh, 1 - c, cross)
         t_send(i, 1, yh, 1 - c, core)
 
-    for d in range(1, NZ):
-
-        @pl.when(rank((z + d) % NZ) < mine)
-        def _():
-            pl.semaphore_signal(here, inc=1, device_id=at_z(d), device_id_type=MESH)
-
     xs_w = (x, xm, xp, x2)
 
     def block(slot, first=False):
@@ -190,6 +190,13 @@
         return remote(
             gsend.at[i - 1], grecv.at[i - 1], ss_g.at[i - 1], rs_g.at[i - 1], device
         )
+
+    whole = (
+        (keys_o, keys_h), (gt_o, gt_h), (dw_o, dw_h), (mom_o, mom_h), (glob_o, glob_h), (syn_o, syn_h),
+    )
+
+    def result(n):
+        return pltpu.make_async_copy(*whole[n], out_sem.at[n])
 
     local[0].wait()
     local[1].wait()
@@ -280,10 +287,6 @@
         else:
             gsend[i - 1] = partial_sum(i).astype(BF16)
             go(g_copy(i))
-
-    c_wait(1)
-    c_wait(3)
-    make_partial(1)
 
     for n in (4, 5, 6):
         local[n].wait()
@@ -332,6 +335,10 @@
     w_fwd(6, 1, 7, left)
     w_fwd(5, 0, 13, core)
     w_fwd(6, 1, 14, core)
+    c_wait(1)
+    c_wait(3)
+    make_partial(1)
+
     make_partial(2)
     w_wait(5, 1)
     w_fwd(5, 1, 13, core)
@@ -359,6 +366,8 @@
     w_wait(15, 1)
     block(15)
     keys_o[...] = (acc[...] * SCALE).astype(BF16)
+    result(0).start()
+    result(1).start()
 
     def hand(j):
         place = (z - 2 * j - odd + NZ) % NZ
@@ -388,6 +397,7 @@
     for n in range(3):
         total = total + grecv[n].astype(F32)
     dw_o[...] = (total * SCALE).astype(BF16)
+    result(2).start()
 
     @pl.when(odd == 1)
     def _():
@@ -396,9 +406,14 @@
 
     mom_o[...] = res[yl, 0]
     glob_o[...] = res[yl, 1]
+    result(3).start()
+    result(4).start()
     for j in range(8):
         taken(j).wait_recv()
-
+    result(5).start()
+
+    for n in range(6):
+        result(n).wait()
     for copy in sent:
         copy.wait_send()
     for j in range(1, 8):
@@ -442,7 +457,15 @@
 
 def on_device(tokens, local_weight, key_cot, global_weight, momentum, anchor):
     dma, vmem = pltpu.SemaphoreType.DMA, pltpu.VMEM
-    scratch = [
+    results = (
+        jax.ShapeDtypeStruct((TOK, KVW), BF16),
+        jax.ShapeDtypeStruct((TOK, 4096), BF16),
+        jax.ShapeDtypeStruct((ROWS, KVW), BF16),
+        jax.ShapeDtypeStruct((8, KVW), F32),
+        jax.ShapeDtypeStruct((8, KVW), F32),
+        jax.ShapeDtypeStruct((16, 16, KVW), BF16),
+    )
+    scratch = [vmem(m.shape, m.dtype) for m in results] + [
         vmem((16, 8, 2, 16, KVW), BF16),
         vmem((TOK, 4096), BF16),
         vmem((4, 4 * TOK, ROWS), BF16),
@@ -469,20 +492,14 @@
         dma((2,)), dma((2,)),
         dma((11,)),
         pltpu.SemaphoreType.REGULAR,
+        dma((6,)),
     ]
-    hbm, in_vmem = pl.BlockSpec(memory_space=pl.ANY), pl.BlockSpec(memory_space=vmem)
+    hbm = pl.BlockSpec(memory_space=pl.ANY)
     made = pl.pallas_call(
         kernel,
-        out_shape=(
-            jax.ShapeDtypeStruct((TOK, KVW), BF16),
-            jax.ShapeDtypeStruct((TOK, 4096), BF16),
-            jax.ShapeDtypeStruct((ROWS, KVW), BF16),
-            jax.ShapeDtypeStruct((8, KVW), F32),
-            jax.ShapeDtypeStruct((8, KVW), F32),
-            jax.ShapeDtypeStruct((16, 16, KVW), BF16),
-        ),
+        out_shape=results,
         in_specs=[hbm] * 6,
-        out_specs=[in_vmem] * 6,
+        out_specs=[hbm] * 6,
         scratch_shapes=scratch,
         compiler_params=pltpu.CompilerParams(
             collective_id=0, has_side_effects=True, vmem_limit_bytes=60 * 2**20

time: 52 us -> 50.9 us (0.979)
  Pallas kernels: 51.2 us -> 50.1 us
    pallas_call x1, Pallas kernels: 48.8 us -> 47.7 us  [on_device(): pl.pallas_call(kernel, out_shape=results, in_specs=[hbm] * 6, out_specs=[...]
where the time goes in v4:
time: 50.9 us; the launch traced here: 50.7 us
  Pallas kernels  50.1 us (98%)
  between operations  0.64 us (1%)
    pallas_call x1, Pallas kernels, on_device(): pl.pallas_call(kernel, out_shape=results, in_specs=[hbm] * 6, out_specs=[...  47.7 us
    pallas_call x1, Pallas kernels, on_device(): pl.pallas_call(write_out, out_shape=tuple((jax.ShapeDtypeStruct(m.shape,...  2.34 us

profile of v4, /device:TPU:1, one launch (start us, length us, event | category | flops | bytes accessed | tf_op | source)
XLA Modules:
  0.0 50.7 jit_solution(11803413017941956070)
XLA Ops:
  0.6 47.7 %step.1 = (bf16[128,512]{1,0:T(8,128)(2,1)}, bf16[128,4096]{1,0:T(8,128)(2,1)}, bf16[256,512]{1,0:T(8,128)(2,1)}, f32[8,512]{1,0:T(8,128)}, f32[8,512]{1,0:T(8,128)}, /*index=5*/bf16[16,16,512]{2,1,0:T(8,128)(2,1)}) custom-call(bf16[128,4096]{1,0:T(8,128)(2,1)} %bitcast.7, bf16[8,2,16,512]{3,2,1,0:T(8,128)(2,1)} %bitcast.9, bf16[128,512]{1,0:T(8,128)(2,1)} %bitcast.12, ...), custom_call_target="tpu_custom_call" | custom-call | flops 1610612736 | bytes 4194304 | tf_op jit(solution)/shard_map/step/pallas_call | solution.py:498
  48.4 2.3 %write_out.1 = (bf16[128,512]{1,0:T(8,128)(2,1)}, bf16[128,4096]{1,0:T(8,128)(2,1)}, bf16[256,512]{1,0:T(8,128)(2,1)}, f32[8,512]{1,0:T(8,128)}, f32[8,512]{1,0:T(8,128)}, /*index=5*/bf16[16,16,512]{2,1,0:T(8,128)(2,1)}) custom-call(bf16[128,512]{1,0:T(8,128)(2,1)} %get-tuple-element.18.refs_0_, bf16[128,4096]{1,0:T(8,128)(2,1)} %get-tuple-element.19.refs_1_, ...), custom_call_target="tpu_custom_call" | custom-call | tf_op jit(solution)/shard_map/write_out/pallas_call | solution.py:519

commit v5 on v4

--- a/solution.py
+++ b/solution.py
@@ -339,6 +339,10 @@
     c_wait(3)
     make_partial(1)
 
+    @pl.when((odd == 0) & jnp.logical_not(late))
+    def _():
+        update()
+
     make_partial(2)
     w_wait(5, 1)
     w_fwd(5, 1, 13, core)
@@ -347,10 +351,6 @@
     block(5)
     block(6)
     make_partial(3)
-
-    @pl.when((odd == 0) & jnp.logical_not(late))
-    def _():
-        update()
 
     for slot in (13, 14):
         w_wait(slot, 0)

time: 50.9 us -> 50.5 us (level)
  no operation moved by 1% of the time
where the time goes in v5:
time: 50.5 us; the launch traced here: 50.4 us
  Pallas kernels  49.7 us (98%)
  between operations  0.64 us (1%)
    pallas_call x1, Pallas kernels, on_device(): pl.pallas_call(kernel, out_shape=results, in_specs=[hbm] * 6, out_specs=[...  47.4 us
    pallas_call x1, Pallas kernels, on_device(): pl.pallas_call(write_out, out_shape=tuple((jax.ShapeDtypeStruct(m.shape,...  2.34 us

profile of v5, /device:TPU:1, one launch (start us, length us, event | category | flops | bytes accessed | tf_op | source)
XLA Modules:
  0.0 50.4 jit_solution(18045581261789350994)
XLA Ops:
  0.6 47.4 %step.1 = (bf16[128,512]{1,0:T(8,128)(2,1)}, bf16[128,4096]{1,0:T(8,128)(2,1)}, bf16[256,512]{1,0:T(8,128)(2,1)}, f32[8,512]{1,0:T(8,128)}, f32[8,512]{1,0:T(8,128)}, /*index=5*/bf16[16,16,512]{2,1,0:T(8,128)(2,1)}) custom-call(bf16[128,4096]{1,0:T(8,128)(2,1)} %bitcast.7, bf16[8,2,16,512]{3,2,1,0:T(8,128)(2,1)} %bitcast.9, bf16[128,512]{1,0:T(8,128)(2,1)} %bitcast.12, ...), custom_call_target="tpu_custom_call" | custom-call | flops 1610612736 | bytes 4194304 | tf_op jit(solution)/shard_map/step/pallas_call | solution.py:498
  48.0 2.3 %write_out.1 = (bf16[128,512]{1,0:T(8,128)(2,1)}, bf16[128,4096]{1,0:T(8,128)(2,1)}, bf16[256,512]{1,0:T(8,128)(2,1)}, f32[8,512]{1,0:T(8,128)}, f32[8,512]{1,0:T(8,128)}, /*index=5*/bf16[16,16,512]{2,1,0:T(8,128)(2,1)}) custom-call(bf16[128,512]{1,0:T(8,128)(2,1)} %get-tuple-element.18.refs_0_, bf16[128,4096]{1,0:T(8,128)(2,1)} %get-tuple-element.19.refs_1_, ...), custom_call_target="tpu_custom_call" | custom-call | tf_op jit(solution)/shard_map/write_out/pallas_call | solution.py:519
